TPU v7x, 512 devices: a whole 4x8x8 slice. The times are simulated.
512 devices in a mesh: seq: 64 (over z, y), head: 8 (over x, core).
Axes of the slice: x: 4, y: 8, z: 8, core: 2. Of those that a mesh axis runs over, the one named last changes fastest.
Arguments:
- queries: bfloat16 [8192, 2048], P('seq', 'head'), may hold values from -6 to 6
- key_vectors: bfloat16 [2, 8192, 2048], P(None, 'seq', 'head'), may hold values from -6 to 6
- values: bfloat16 [2, 8192, 2048], P(None, 'seq', 'head'), may hold values from -6 to 6
- strengths: float32 [2, 16, 8192], P(None, 'head', 'seq'), may hold values from 0.05 to 1.95
- out_weight: bfloat16 [2048, 4096], P('head', 'seq'), may hold values from -0.375 to 0.375
Outputs:
- mixed: bfloat16 [8192, 4096], P('seq', 'head')
All inputs are finite; a program needn't handle non-finite values.
Results may differ from a plain program's by a relative error of at most 0.014.
Values may be sent and summed in bfloat16 or wider, within the bound.
A program may use at most 64 MiB of HBM per device.

v0:
```python
import jax
import jax.numpy as jnp
from jax import lax
from jax.sharding import PartitionSpec as P

BLOCK = 64


HIGHEST_PRECISION = lax.Precision.HIGHEST


def carried_in(value, axis, join, neutral):
    count, mine = (lax.axis_size(axis), lax.axis_index(axis))
    pieces = jax.tree.map(lambda part: lax.all_gather(part, axis), value)
    total = jax.tree.map(
        lambda part, zero: jnp.full_like(part, 0) + jnp.asarray(zero, part.dtype), value, neutral
    )

    def hop(position, total):
        longer = join(total, jax.tree.map(lambda part: part[position], pieces))
        return jax.tree.map(lambda new, old: jnp.where(position < mine, new, old), longer, total)

    return lax.fori_loop(0, count - 1, hop, total)


def unit_rows(matrix):
    return matrix * lax.rsqrt(jnp.sum(matrix * matrix, axis=-1, keepdims=True) + 1e-06)


def block_inputs(inputs, first_row):
    queries, key_vectors, values, strengths = inputs
    head_count = strengths.shape[1]
    head_width = queries.shape[1] // head_count
    query_part = (
        lax.dynamic_slice_in_dim(queries, first_row, BLOCK, 0)
        .astype(jnp.float32)
        .reshape(BLOCK, head_count, head_width)
    )
    key_part = (
        lax.dynamic_slice_in_dim(key_vectors, first_row, BLOCK, 1)
        .astype(jnp.float32)
        .reshape(2, BLOCK, head_count, head_width)
    )
    value_part = (
        lax.dynamic_slice_in_dim(values, first_row, BLOCK, 1)
        .astype(jnp.float32)
        .reshape(2, BLOCK, head_count, head_width)
    )
    beta_part = lax.dynamic_slice_in_dim(strengths, first_row, BLOCK, 2)
    query_heads = jnp.transpose(unit_rows(query_part), (1, 0, 2))
    key_heads = jnp.transpose(unit_rows(key_part), (2, 1, 0, 3)).reshape(
        head_count, 2 * BLOCK, head_width
    )
    value_heads = jnp.transpose(value_part, (2, 1, 0, 3)).reshape(head_count, 2 * BLOCK, head_width)
    beta_heads = jnp.transpose(beta_part, (1, 2, 0)).reshape(head_count, 2 * BLOCK)
    return (query_heads, key_heads, value_heads, beta_heads)


def solve_block(key_heads, right_side, beta_heads):
    key_gram = jnp.einsum("hik,hjk->hij", key_heads, key_heads, precision=HIGHEST_PRECISION)
    system = jnp.tril(key_gram, -1) * beta_heads[:, :, None] + jnp.eye(2 * BLOCK, dtype=jnp.float32)
    return jax.scipy.linalg.solve_triangular(
        system, beta_heads[:, :, None] * right_side, lower=True, unit_diagonal=True
    )


def reach_table():
    row_ids = lax.broadcasted_iota(jnp.int32, (BLOCK, 2 * BLOCK), 0)
    col_ids = lax.broadcasted_iota(jnp.int32, (BLOCK, 2 * BLOCK), 1)
    return (col_ids <= 2 * row_ids + 1).astype(jnp.float32)


def compose(earlier, later):
    product = jnp.einsum("hjk,hkl->hjl", earlier[0], later[0], precision=HIGHEST_PRECISION)
    state = jnp.einsum("hjk,hkl->hjl", earlier[1], later[0], precision=HIGHEST_PRECISION) + later[1]
    return (product, state)


def incoming_state(product, local_state, identity_stack, zero_state):
    prefix = carried_in((product, local_state), "seq", compose, (identity_stack, zero_state))
    return prefix[1]


def per_device(queries, key_vectors, values, strengths, out_weight):
    head_count = strengths.shape[1]
    tok_rows = queries.shape[0]
    head_width = queries.shape[1] // head_count
    inputs = (queries, key_vectors, values, strengths)
    first_rows = jnp.arange(tok_rows // BLOCK, dtype=jnp.int32) * BLOCK
    identity_stack = jnp.broadcast_to(
        jnp.eye(head_width, dtype=jnp.float32), (head_count, head_width, head_width)
    )
    zero_state = jnp.zeros((head_count, head_width, head_width), jnp.float32)
    reach_mask = reach_table()

    def carry_step(carried, first_row):
        local_state, product = carried
        query_heads, key_heads, value_heads, beta_heads = block_inputs(inputs, first_row)
        solved = solve_block(
            key_heads, jnp.concatenate([key_heads, value_heads], axis=2), beta_heads
        )
        shrink = identity_stack - jnp.einsum(
            "hik,hil->hkl", solved[:, :, :head_width], key_heads, precision=HIGHEST_PRECISION
        )
        growth = jnp.einsum(
            "hiv,hik->hvk", solved[:, :, head_width:], key_heads, precision=HIGHEST_PRECISION
        )
        local_state = (
            jnp.einsum("hvk,hkl->hvl", local_state, shrink, precision=HIGHEST_PRECISION) + growth
        )
        product = jnp.einsum("hjk,hkl->hjl", product, shrink, precision=HIGHEST_PRECISION)
        return ((local_state, product), None)

    (local_state, product), unused = lax.scan(carry_step, (zero_state, identity_stack), first_rows)
    state_in = incoming_state(product, local_state, identity_stack, zero_state)

    def replay_step(state, first_row):
        query_heads, key_heads, value_heads, beta_heads = block_inputs(inputs, first_row)
        right_side = value_heads - jnp.einsum(
            "hik,hvk->hiv", key_heads, state, precision=HIGHEST_PRECISION
        )
        updates = solve_block(key_heads, right_side, beta_heads)
        scores = (
            jnp.einsum("htk,hik->hti", query_heads, key_heads, precision=HIGHEST_PRECISION)
            * reach_mask
        )
        block_out = jnp.einsum(
            "hvk,htk->htv", state, query_heads, precision=HIGHEST_PRECISION
        ) + jnp.einsum("hti,hiv->htv", scores, updates, precision=HIGHEST_PRECISION)
        new_state = state + jnp.einsum(
            "hiv,hik->hvk", updates, key_heads, precision=HIGHEST_PRECISION
        )
        return (new_state, block_out)

    final_state, heads_out = lax.scan(replay_step, state_in, first_rows)
    mixed_heads = (
        jnp.transpose(heads_out, (0, 2, 1, 3))
        .reshape(tok_rows, head_count * head_width)
        .astype(jnp.bfloat16)
    )
    partial_sums = jnp.dot(
        mixed_heads,
        lax.all_gather(out_weight, "seq", axis=1, tiled=True),
        preferred_element_type=jnp.float32,
    )
    return lax.psum_scatter(
        partial_sums.astype(jnp.bfloat16), "head", scatter_dimension=1, tiled=True
    )


def solution(mesh):
    return jax.shard_map(
        per_device,
        mesh=mesh,
        in_specs=(
            P("seq", "head"),
            P(None, "seq", "head"),
            P(None, "seq", "head"),
            P(None, "head", "seq"),
            P("head", "seq"),
        ),
        out_specs=P("seq", "head"),
        check_vma=False,
    )
```

profile of v0, /device:TPU:8, one launch (start us, length us, event | category | flops | bytes accessed | tf_op | source)
XLA Modules:
  0.0 516.8 jit_solution(7215784135257742061)
XLA Ops:
  7.5 53.9 %while.41 = (s32[]{:T(128)}, f32[2,128,128]{1,2,0:T(8,128)S(1)}, f32[2,128,128]{1,2,0:T(8,128)S(1)}, s32[2]{0:T(128)S(1)}, bf16[2,128,256]{2,1,0:T(8,128)(2,1)},...) while((s32[]{:T(128)}, f32[2,128,128]{1,2,0:T(8,128)S(1)}, ...), condition=%wide.region_2.3_spmd.clone, body=%wide.region_0.2_spmd.clone.sunk | while | flops 352960640 | bytes 5352621 | solution.py:114
  12.5 19.7 %custom-call.16 = f32[2,1,128,128]{2,3,1,0:T(8,128)S(1)} custom-call(f32[2,1,128,128]{3,2,1,0:T(8,128)S(1)} %fusion.145), custom_call_target="InvertDiagBlocksLowerTriangular" | custom-call | tf_op jit(solution)/shard_map/while/body/eval_jaxpr/jit(_solve_triangular)/vmap()/triangular_solve | solution.py:62
  39.5 19.7 %custom-call.16 = f32[2,1,128,128]{2,3,1,0:T(8,128)S(1)} custom-call(f32[2,1,128,128]{3,2,1,0:T(8,128)S(1)} %fusion.145), custom_call_target="InvertDiagBlocksLowerTriangular" | custom-call | tf_op jit(solution)/shard_map/while/body/eval_jaxpr/jit(_solve_triangular)/vmap()/triangular_solve | solution.py:62
  64.1 102.2 %all-gather.8.cloned.1.call-done = f32[128,128,128]{2,1,0:T(8,128)} async-done(((f32[2,128,128]{2,1,0:T(8,128)}), f32[128,128,128]{2,1,0:T(8,128)}) %all-gather.8.cloned.1.call-update) | async-done | bytes 8388624 | tf_op jit(solution)/shard_map/all_gather | solution.py:14
  166.3 100.5 %all-gather.10.cloned.1.call-done = f32[128,128,128]{2,1,0:T(8,128)} async-done(((f32[2,128,128]{2,1,0:T(8,128)}), f32[128,128,128]{2,1,0:T(8,128)}) %all-gather.10.cloned.1.call-update) | async-done | bytes 8388624 | tf_op jit(solution)/shard_map/all_gather | solution.py:14
  266.8 149.8 %while.42 = (s32[]{:T(128)}, f32[2,128,128]{1,2,0:T(8,128)S(1)}, s32[]{:T(128)}, f32[64,2,128,128]{3,2,1,0:T(8,128)}, f32[64,2,128,128]{3,2,1,0:T(8,128)}, /*index=5*/s32[]{:T(128)}, s32[]{:T(128)}) while((s32[]{:T(128)}, f32[2,128,128]{1,2,0:T(8,128)S(1)}, s32[]{:T(128)}, f32[64,2,128,128]{3,2,1,0:T(8,128)}, ...), condition=%wide.region_4.5_spmd.clone, body=%wide.region_3.4_spmd.clone.sunk | while | flops 50462724 | bytes 1443939 | solution.py:23
  267.9 1.3 fusion.151
  270.3 1.3 fusion.151
  272.6 1.3 fusion.151
  275.0 1.3 fusion.151
  277.4 1.3 fusion.151
  279.8 1.3 fusion.151
  282.1 1.3 fusion.151
  284.5 1.3 fusion.151
  286.9 1.3 fusion.151
  289.3 1.3 fusion.151
  291.7 1.3 fusion.151
  294.0 1.3 fusion.151
  296.4 1.3 fusion.151
  298.8 1.3 fusion.151
  301.2 1.3 fusion.151
  303.5 1.3 fusion.151
  305.9 1.3 fusion.151
  308.3 1.3 fusion.151
  310.7 1.3 fusion.151
  313.1 1.3 fusion.151
  315.4 1.3 fusion.151
  317.8 1.3 fusion.151
  320.2 1.3 fusion.151
  322.6 1.3 fusion.151
  324.9 1.3 fusion.151
  327.3 1.3 fusion.151
  329.7 1.3 fusion.151
  332.1 1.3 fusion.151
  334.5 1.3 fusion.151
  336.8 1.3 fusion.151
  339.2 1.3 fusion.151
  341.6 1.3 fusion.151
  344.0 1.3 fusion.151
  346.4 1.3 fusion.151
  348.7 1.3 fusion.151
  353.5 1.3 fusion.151
  358.2 1.3 fusion.151
  360.6 1.3 fusion.151
  367.7 1.3 fusion.151
  370.1 1.3 fusion.151
  372.5 1.3 fusion.151
  379.6 1.3 fusion.151
  382.0 1.3 fusion.151
  389.1 1.3 fusion.151
  391.5 1.3 fusion.151
  393.9 1.3 fusion.151
  398.6 1.3 fusion.151
  401.0 1.3 fusion.151
  403.4 1.3 fusion.151
  405.8 1.3 fusion.151
  410.5 1.3 fusion.151
  412.9 1.3 fusion.151
  415.3 1.3 fusion.151
  416.7 54.6 %while.40 = (s32[]{:T(128)}, f32[2,128,128]{2,1,0:T(8,128)S(1)}, bf16[2,2,64,128]{3,2,1,0:T(8,128)(2,1)S(1)}, s32[2]{0:T(128)S(1)}, bf16[2,128,256]{2,1,0:T(8,12...) while((s32[]{:T(128)}, f32[2,128,128]{2,1,0:T(8,128)S(1)}, ...), condition=%wide.region_8.9_spmd.clone, body=%wide.region_5.8_spmd.clone.sunk | while | flops 277446784 | bytes 5191091 | solution.py:135
  421.5 19.7 %custom-call.15 = f32[2,1,128,128]{2,3,1,0:T(8,128)S(1)} custom-call(f32[2,1,128,128]{3,2,1,0:T(8,128)S(1)} %fusion.128), custom_call_target="InvertDiagBlocksLowerTriangular" | custom-call | tf_op jit(solution)/shard_map/while/body/eval_jaxpr/jit(_solve_triangular)/vmap()/triangular_solve | solution.py:62
  448.8 19.7 %custom-call.15 = f32[2,1,128,128]{2,3,1,0:T(8,128)S(1)} custom-call(f32[2,1,128,128]{3,2,1,0:T(8,128)S(1)} %fusion.128), custom_call_target="InvertDiagBlocksLowerTriangular" | custom-call | tf_op jit(solution)/shard_map/while/body/eval_jaxpr/jit(_solve_triangular)/vmap()/triangular_solve | solution.py:62
  471.4 3.4 convolution_convert_fusion
  474.8 35.5 %reduce-scatter.2.cloned.1.call-done = bf16[128,512]{1,0:T(8,128)(2,1)} async-done(((bf16[128,4096]{1,0:T(8,128)(2,1)}), bf16[128,512]{1,0:T(8,128)(2,1)}) %reduce-scatter.2.cloned.1.call-update) | async-done | bytes 131088 | tf_op jit(solution)/shard_map/reduce_scatter | solution.py:146
  (321 shorter events, 102.3 us)
Async XLA Ops:
  6.5 159.8 %all-gather.8.cloned.1.call-start = ((), (), s32[]{:S(2)}) async-start(), calls=%async_computation.3 | async-start | bytes 8519680 | tf_op jit(solution)/shard_map/all_gather | solution.py:14
  7.5 409.2 %copy-start = (bf16[128,256]{1,0:T(8,128)(2,1)S(1)}, bf16[128,256]{1,0:T(8,128)(2,1)}, u32[]{:S(2)}) copy-start(bf16[128,256]{1,0:T(8,128)(2,1)} %param.11) | copy-start | bytes 196612
  62.2 204.6 %all-gather.10.cloned.1.call-start = ((), (), s32[]{:S(2)}) async-start(), calls=%async_computation.4 | async-start | bytes 8519680 | tf_op jit(solution)/shard_map/all_gather | solution.py:14
  63.1 408.4 %all-gather.6.cloned.1.call-start = ((), (), s32[]{:S(2)}) async-start(), calls=%async_computation.1 | async-start | bytes 2129920 | tf_op jit(solution)/shard_map/all_gather | solution.py:143
  63.8 446.5 %reduce-scatter.2.cloned.1.call-start = ((), (), s32[]{:S(2)}) async-start(), calls=%async_computation.2 | async-start | bytes 1179648 | tf_op jit(solution)/shard_map/reduce_scatter | solution.py:146
Sparse Core Ops, SparseCore 0:
  62.4 103.8 all-gather.7
  169.4 97.4 all-gather.9
  269.9 81.3 all-gather.5
  475.0 35.2 reduce-scatter.1
where the time goes:
time: 520 us; the launch traced here: 517 us
  waiting for transfers between devices  239 us (46%)
  matrix products  95.5 us (18%)
  other arithmetic  85.3 us (16%)
  local copies, waits for them, and re-layouts  71.7 us (14%)
  between operations  13.3 us (3%)
  loops' own time  11.8 us (2%)
    all_gather x2, waiting for transfers between devices, carried_in(): pieces = jax.tree.map(lambda part: lax.all_gather(part, axis), value)  203 us
    dot_general x63, matrix products, compose(): jnp.einsum('hjk,hkl->hjl', earlier[1], later[0], precision=HIGHEST_PRECIS...  82.2 us
    another operation x16, other arithmetic, solve_block(): jax.scipy.linalg.solve_triangular(system, beta_heads[:, :, None] * right_...  79.1 us
    dynamic_slice x126, local copies, waits for them, and re-layouts, hop(): longer = join(total, jax.tree.map(lambda part: part[position], pieces))  63.8 us
    reduce_scatter x1, waiting for transfers between devices, per_device(): lax.psum_scatter(partial_sums.astype(jnp.bfloat16), 'head', scatter_dimen...  35.5 us
  transfers between devices with their start and end apart: 4, of which 3 were waited for; matrix products, arithmetic and copies ran while one was open for 38% of the time, Pallas kernels for 0%

commit v1 on v0

v1 whole, which is shorter than its diff:
```python
import functools

import jax
import jax.numpy as jnp
from jax import lax
from jax.experimental import pallas as pl
from jax.experimental.pallas import tpu as pltpu
from jax.sharding import PartitionSpec as P

MESH = pl.DeviceIdType.MESH
F32 = jnp.float32
BF16 = jnp.bfloat16


def dot(a, b):
    return jnp.dot(a, b, preferred_element_type=F32)


def dot_nt(a, b):
    return lax.dot_general(a, b, (((1,), (1,)), ((), ())), preferred_element_type=F32)


def dot_tn(a, b):
    return lax.dot_general(a, b, (((0,), (0,)), ((), ())), preferred_element_type=F32)


def split(a):
    high = a.astype(BF16)
    return high, (a - high.astype(F32)).astype(BF16)


def dot3(a, b):
    return dot(a[0], b[0]) + (dot(a[1], b[0]) + dot(a[0], b[1]))


class Ring:
    def __init__(self, n, place, device_at, slot, send, recv):
        self.n, self.place, self.device_at, self.slot = n, place, device_at, slot
        self.send, self.recv = send, recv

    def parts(self, hop, way):
        return (way,) if hop == self.n // 2 - 1 else (0, 1)

    def copy(self, hop, way, part, arriving):
        n, sign = self.n, (1, -1)[way]
        owner = lax.rem(self.place + 2 * n - sign * (hop + arriving), n)
        block = self.slot(owner, part)
        return pltpu.make_async_remote_copy(
            src_ref=block,
            dst_ref=block,
            send_sem=self.send.at[way, hop, part],
            recv_sem=self.recv.at[way, hop, part],
            device_id=self.device_at(lax.rem(self.place + n + sign, n)),
            device_id_type=MESH,
        )

    def hop(self, hop):
        for part in (0, 1):
            for way in (0, 1):
                if hop > 0 and part in self.parts(hop - 1, way):
                    self.copy(hop - 1, way, part, 1).wait_recv()
                if hop < self.n // 2 and part in self.parts(hop, way):
                    self.copy(hop, way, part, 0).start()

    def finish(self):
        for hop in range(self.n // 2):
            for way in (0, 1):
                for part in self.parts(hop, way):
                    self.copy(hop, way, part, 0).wait_send()


def kernel(
    nz, ny, nh,
    q_ref, k_ref, v_ref, b_ref, w_ref, o_ref,
    k_int, v_int, wt, wa, wb, d_all, g_out, g_in, m_all, e_all, s_pre, s_out, s_in, h_all,
    wt_send, wt_recv, wa1_send, wa1_recv, wb1_send, wb1_recv, wa2_send, wa2_recv, wb2_send, wb2_recv,
    d_send, d_recv, g_send, g_recv, m_send, m_recv, s_send, s_recv, x_send, x_recv, c_send, c_recv,
):
    seq, head = lax.axis_index("seq"), lax.axis_index("head")
    z, y = seq // ny, lax.rem(seq, ny)
    x, core = head // 2, lax.rem(head, 2)
    nx = nh // 2
    heads = b_ref.shape[1]
    toks = q_ref.shape[0]
    dk = q_ref.shape[1] // heads
    refl = 2 * toks
    sl = dk // ny
    off_diagonal = z != head

    barrier = pltpu.get_barrier_semaphore()
    partners = [(z * ny + lax.rem(y + d, ny), head) for d in range(1, ny)]
    z_ring = {1, nz - 1}
    partners += [(lax.rem(z + d, nz) * ny + y, head) for d in sorted(z_ring)]
    x_ring = {1, nx - 1} - {0}
    partners += [(seq, lax.rem(x + d, nx) * 2 + core) for d in sorted(x_ring)]
    partners += [(seq, x * 2 + 1 - core)]
    for partner in partners:
        pl.semaphore_signal(barrier, inc=1, device_id=partner, device_id_type=MESH)

    @pl.when(off_diagonal)
    def _():
        pl.semaphore_signal(
            barrier, inc=1, device_id=(head * ny + y, z), device_id_type=MESH
        )

    def enter():
        pl.semaphore_wait(barrier, len(partners) + off_diagonal.astype(jnp.int32))

    def turned(half, dst):
        return pltpu.make_async_remote_copy(
            src_ref=wt.at[half],
            dst_ref=dst,
            send_sem=wt_send.at[half],
            recv_sem=wt_recv.at[half],
            device_id=(head * ny + y, z),
            device_id_type=MESH,
        )

    cols = w_ref.shape[1]
    eye_cols = (
        lax.broadcasted_iota(jnp.int32, (cols, cols), 0)
        == lax.broadcasted_iota(jnp.int32, (cols, cols), 1)
    ).astype(BF16)
    for half in (0, 1):
        wt[half] = dot_nt(eye_cols, w_ref[half * dk : (half + 1) * dk, :]).astype(BF16)

    def send_turned():
        @pl.when(off_diagonal)
        def _():
            turned(0, wa.at[head, y]).start()
            turned(1, wb.at[y, head]).start()

        @pl.when(jnp.logical_not(off_diagonal))
        def _():
            wa[z, y] = wt[0]
            wb[y, z] = wt[1]

    def take_turned():
        @pl.when(off_diagonal)
        def _():
            turned(0, wa.at[z, y]).wait_recv()
            turned(1, wb.at[y, z]).wait_recv()

    def on_y(i):
        return (z * ny + i, head)

    def on_z(i):
        return (i * ny + y, head)

    def on_x(i):
        return (seq, i * 2 + core)

    half_cols = cols // 2

    def rows(part):
        return pl.ds(part * half_cols, half_cols)

    wa1 = Ring(ny, y, on_y, lambda i, p: wa.at[z, i, rows(p)], wa1_send, wa1_recv)
    wb1 = Ring(nz, z, on_z, lambda i, p: wb.at[y, i, rows(p)], wb1_send, wb1_recv)
    wa2 = Ring(nz, z, on_z, lambda i, p: wa.at[i, pl.ds(p * (ny // 2), ny // 2)], wa2_send, wa2_recv)
    wb2 = Ring(ny, y, on_y, lambda i, p: wb.at[i, pl.ds(p * (nz // 2), nz // 2)], wb2_send, wb2_recv)
    d_ring = Ring(ny, y, on_y, lambda i, p: d_all.at[i, p], d_send, d_recv)
    m_ring = Ring(nz, z, on_z, lambda i, p: m_all.at[i, p], m_send, m_recv)
    x_rg = Ring(nx, x, on_x, lambda i, p: h_all.at[i * 2 + core, p], x_send, x_recv)

    def to_y(d, out, into, send, recv, arriving):
        peer = lax.rem(y + d, ny)
        other = lax.rem(y + ny - d, ny)
        return pltpu.make_async_remote_copy(
            src_ref=out.at[other if arriving else peer],
            dst_ref=into.at[other if arriving else y],
            send_sem=send.at[d],
            recv_sem=recv.at[d],
            device_id=on_y(peer),
            device_id_type=MESH,
        )

    enter()
    send_turned()

    tok_id = lax.broadcasted_iota(jnp.int32, (refl, toks), 1)
    row_of = lax.broadcasted_iota(jnp.int32, (refl, toks), 0)
    ri = lax.broadcasted_iota(jnp.int32, (refl, refl), 0)
    ci = lax.broadcasted_iota(jnp.int32, (refl, refl), 1)
    keys, systems, inverses, sides = [], [], [], []
    for h in range(heads):
        cut = slice(h * dk, (h + 1) * dk)
        for j in (0, 1):
            k_int[h, pl.ds(j, toks, stride=2), :] = k_ref[j, :, cut].astype(F32)
            v_int[h, pl.ds(j, toks, stride=2), :] = v_ref[j, :, cut].astype(F32)
    for h in range(heads):
        key = k_int[h]
        inv = lax.rsqrt(jnp.sum(key * key, axis=1, keepdims=True) + 1e-06)
        picked = jnp.where(
            lax.rem(row_of, 2) == 0, b_ref[0, h : h + 1, :], b_ref[1, h : h + 1, :]
        )
        beta = jnp.sum(jnp.where(row_of // 2 == tok_id, picked, 0.0), axis=1, keepdims=True)
        beta_inv = beta * inv
        gain = beta_inv * inv
        kb = key.astype(BF16)
        keys.append(kb)
        systems.append(jnp.where(ri > ci, gain * dot_nt(kb, kb), 0.0))
        sides.append(jnp.concatenate([gain * key, beta_inv * v_int[h]], axis=1))
    eye = (ri == ci).astype(F32)
    inverses = [eye - jnp.where((ri >> 1) == (ci >> 1), a, 0.0) for a in systems]
    level = 1
    background = {2: [take_turned, lambda: wa1.hop(0), lambda: wb1.hop(0)]}
    for step in range(1, ny // 2 + 1):
        background.setdefault(2 + step, []).append(functools.partial(wa1.hop, step))
    for step in range(1, nz // 2 + 1):
        background.setdefault(2 + step, []).append(functools.partial(wb1.hop, step))
    while (1 << level) < refl:
        here = ((ri >> (level + 1)) == (ci >> (level + 1))) & ((ri >> level) != (ci >> level))
        for h in range(heads):
            xb = inverses[h].astype(BF16)
            inner = dot(jnp.where(here, systems[h], 0.0).astype(BF16), xb)
            inverses[h] = inverses[h] - dot(xb, inner.astype(BF16))
        for act in background.pop(level, []):
            act()
        level += 1
    for left in sorted(background):
        for act in background[left]:
            act()
    wa2.hop(0)
    solved = []
    for h in range(heads):
        xs = split(inverses[h])
        residual = (eye - inverses[h]) - dot3(split(systems[h]), xs)
        fine = split(inverses[h] + dot(xs[0], residual.astype(BF16)))
        solved.append(dot3(fine, split(sides[h])))
    for h in range(heads):
        sh, slo = split(solved[h])
        moved = dot_tn(sh, keys[h]) + dot_tn(slo, keys[h])
        d_all[y, h] = moved[:dk].astype(BF16)
        g_out[:, h] = moved[dk:].astype(BF16).reshape(ny, sl, dk)
    d_ring.hop(0)
    for d in range(1, ny):
        to_y(d, g_out, g_in, g_send, g_recv, 0).start()
    g_in[y] = g_out[y]

    reach = (
        lax.broadcasted_iota(jnp.int32, (toks, refl), 1)
        <= 2 * lax.broadcasted_iota(jnp.int32, (toks, refl), 0) + 1
    )
    reads, locals_, q_inv = [], [], []

    def read_head(h):
        qb = q_ref[:, h * dk : (h + 1) * dk]
        qf = qb.astype(F32)
        q_inv.append(lax.rsqrt(jnp.sum(qf * qf, axis=1, keepdims=True) + 1e-06))
        scores = jnp.where(reach, dot_nt(qb, keys[h]), 0.0)
        both = dot3(split(scores), split(solved[h]))
        reads.append((qf - both[:, :dk]).astype(BF16))
        locals_.append(both[:, dk:])

    for step in range(max(heads, ny // 2)):
        if step < heads:
            read_head(step)
        if step < ny // 2:
            d_ring.hop(step + 1)
    for d in range(1, ny):
        to_y(d, g_out, g_in, g_send, g_recv, 1).wait_recv()

    top = (
        lax.broadcasted_iota(jnp.int32, (dk + sl, dk), 0)
        == lax.broadcasted_iota(jnp.int32, (dk + sl, dk), 1)
    ).astype(F32)
    stack = [jnp.zeros((dk + sl, dk), F32) for _ in range(heads)]
    pad = jnp.zeros((dk, dk), F32)
    for i in range(ny):
        for h in range(heads):
            e_all[h, :, i * dk : (i + 1) * dk] = stack[h][:dk].astype(BF16)
            s_pre[i, h] = stack[h][dk:]
            grown = jnp.concatenate([pad, g_in[i, h].astype(F32)], axis=0)
            stack[h] = stack[h] + dot((top - stack[h]).astype(BF16), d_all[i, h]) + grown
    for h in range(heads):
        m_all[z, h] = stack[h].astype(BF16)
    m_ring.hop(0)
    wa2.hop(1)
    wb2.hop(0)
    for step in range(1, nz // 2 + 1):
        m_ring.hop(step)
    state = [jnp.zeros((sl, dk), F32) for _ in range(heads)]
    for i in range(nz - 1):
        for h in range(heads):
            after = state[h] - dot(state[h].astype(BF16), m_all[i, h, :dk]) + m_all[i, h, dk:].astype(F32)
            state[h] = jnp.where(i < z, after, state[h])
    for h in range(heads):
        drop = dot(state[h].astype(BF16), e_all[h])
        for i in range(ny):
            s_out[i, h] = (state[h] - drop[:, i * dk : (i + 1) * dk] + s_pre[i, h]).astype(BF16)
    for d in range(1, ny):
        to_y(d, s_out, s_in, s_send, s_recv, 0).start()
    s_in[y] = s_out[y]
    for step in range(2, nz // 2 + 1):
        wa2.hop(step)
    for step in range(1, ny // 2 + 1):
        wb2.hop(step)
    for d in range(1, ny):
        to_y(d, s_out, s_in, s_send, s_recv, 1).wait_recv()
    for h in range(heads):
        carried = s_in[:, h].reshape(dk, dk)
        h_all[head, h] = (q_inv[h] * (dot_nt(reads[h], carried) + locals_[h])).astype(BF16)

    def across(i, h, arriving):
        block = h_all.at[i * 2 + (1 - core if arriving else core), h]
        return pltpu.make_async_remote_copy(
            src_ref=block,
            dst_ref=block,
            send_sem=c_send.at[i, h],
            recv_sem=c_recv.at[i, h],
            device_id=(seq, x * 2 + 1 - core),
            device_id_type=MESH,
        )

    if nx > 1:
        x_rg.hop(0)
        for step in range(1, nx // 2 + 1):
            x_rg.hop(step)
    for i in range(nx):
        for h in range(heads):
            across(i, h, 0).start()
    total = None
    for i in range(nx):
        for h in range(heads):
            across(i, h, 1).wait_recv()
    for i in range(nh):
        left = jnp.concatenate([h_all[i, h] for h in range(heads)], axis=1)
        right = jnp.concatenate(
            [wa[i].reshape(ny * cols, dk), wb[:, i].reshape(ny * cols, dk)], axis=1
        )
        term = dot_nt(left, right)
        total = term if total is None else total + term
    o_ref[...] = total.astype(BF16)

    @pl.when(off_diagonal)
    def _():
        turned(0, wa.at[head, y]).wait_send()
        turned(1, wb.at[y, head]).wait_send()

    for ring in (wa1, wb1, wa2, wb2, d_ring, m_ring) + ((x_rg,) if nx > 1 else ()):
        ring.finish()
    for d in range(1, ny):
        to_y(d, g_out, g_in, g_send, g_recv, 0).wait_send()
        to_y(d, s_out, s_in, s_send, s_recv, 0).wait_send()
    for i in range(nx):
        for h in range(heads):
            across(i, h, 0).wait_send()


def solution(mesh):
    nh = mesh.shape["head"]
    nz = nh
    ny = mesh.shape["seq"] // nz
    nx = nh // 2

    def per_device(queries, key_vectors, values, strengths, out_weight):
        toks = queries.shape[0]
        heads = strengths.shape[1]
        dk = queries.shape[1] // heads
        cols = out_weight.shape[1]
        sl = dk // ny
        vmem, dma = pltpu.VMEM, pltpu.SemaphoreType.DMA

        def ring(n):
            return [dma((2, max(n // 2, 1), 2))] * 2

        return pl.pallas_call(
            functools.partial(kernel, nz, ny, nh),
            out_shape=jax.ShapeDtypeStruct((toks, ny * cols), BF16),
            in_specs=[pl.BlockSpec(memory_space=pltpu.VMEM)] * 5,
            out_specs=pl.BlockSpec(memory_space=pltpu.VMEM),
            scratch_shapes=[
                vmem((heads, 2 * toks, dk), F32),
                vmem((heads, 2 * toks, dk), F32),
                vmem((2, cols, dk), BF16),
                vmem((nz, ny, cols, dk), BF16),
                vmem((ny, nz, cols, dk), BF16),
                vmem((ny, heads, dk, dk), BF16),
                vmem((ny, heads, sl, dk), BF16),
                vmem((ny, heads, sl, dk), BF16),
                vmem((nz, heads, dk + sl, dk), BF16),
                vmem((heads, dk, ny * dk), BF16),
                vmem((ny, heads, sl, dk), F32),
                vmem((ny, heads, sl, dk), BF16),
                vmem((ny, heads, sl, dk), BF16),
                vmem((nh, heads, toks, dk), BF16),
                dma((2,)),
                dma((2,)),
                *ring(ny),
                *ring(nz),
                *ring(nz),
                *ring(ny),
                *ring(ny),
                dma((ny,)),
                dma((ny,)),
                *ring(nz),
                dma((ny,)),
                dma((ny,)),
                *ring(nx),
                dma((nx, heads)),
                dma((nx, heads)),
            ],
            compiler_params=pltpu.CompilerParams(
                collective_id=0, has_side_effects=True, vmem_limit_bytes=48 * 1024 * 1024
            ),
        )(queries, key_vectors, values, strengths, out_weight)

    return jax.shard_map(
        per_device,
        mesh=mesh,
        in_specs=(
            P("seq", "head"),
            P(None, "seq", "head"),
            P(None, "seq", "head"),
            P(None, "head", "seq"),
            P("head", "seq"),
        ),
        out_specs=P("seq", "head"),
        check_vma=False,
    )
```

time: 520 us -> 99.1 us (0.19)
  the two profiles are of different devices: /device:TPU:8 before, /device:TPU:7 now
where the time goes in v1:
time: 99.1 us; the launch traced here: 98.9 us
  Pallas kernels  95.5 us (96%)
  local copies, waits for them, and re-layouts  3.37 us (3%)
    pallas_call x1, Pallas kernels, per_device(): pl.pallas_call(functools.partial(kernel, nz, ny, nh), out_shape=jax.Shape...  95.5 us
    unnamed x10, local copies, waits for them, and re-layouts  3.37 us

profile of v1, /device:TPU:7, one launch (start us, length us, event | category | flops | bytes accessed | tf_op | source)
XLA Modules:
  0.0 98.9 jit_solution(3815179785696437218)
XLA Ops:
  0.0 0.0 copy-start.3
  0.0 0.0 copy-start.2
  0.0 0.9 copy.6.w_ref
  0.9 0.0 copy-done.3
  0.9 0.0 copy-done.2
  0.9 0.0 copy-start
  0.9 0.9 copy-done
  1.8 0.0 copy-start.1
  1.8 0.9 copy-done.1
  2.7 95.5 %shard_map.55 = bf16[128,512]{1,0:T(8,128)(2,1)S(1)} custom-call(bf16[128,256]{1,0:T(8,128)(2,1)S(1)} %copy-done.2, bf16[2,128,256]{2,1,0:T(8,128)(2,1)S(1)} %copy-done, bf16[2,128,256]{2,1,0:T(8,128)(2,1)S(1)} %copy-done.1, f32[2,2,128]{2,1,0:T(2,128)S(1)} %copy-done.3, bf16[256,64]{1,0:T(8,128)(2,1)S(1)} %copy.6.w_ref), custom_call_target="tpu_custom_call" | custom-call | tf_op jit(solution)/shard_map/pallas_call | solution.py:368
  98.3 0.7 copy.8
Async XLA Ops:
  0.0 0.9 copy-start.3
  0.0 0.9 copy-start.2
  0.9 0.9 copy-start
  1.8 0.9 copy-start.1

commit v2 on v1

v2 whole, which is shorter than its diff:
```python
import functools

import jax
import jax.numpy as jnp
from jax import lax
from jax.experimental import pallas as pl
from jax.experimental.pallas import tpu as pltpu
from jax.sharding import PartitionSpec as P

MESH = pl.DeviceIdType.MESH
F32 = jnp.float32
BF16 = jnp.bfloat16


def dot(a, b):
    return jnp.dot(a, b, preferred_element_type=F32)


def dot_nt(a, b):
    return lax.dot_general(a, b, (((1,), (1,)), ((), ())), preferred_element_type=F32)


def dot_tn(a, b):
    return lax.dot_general(a, b, (((0,), (0,)), ((), ())), preferred_element_type=F32)


def split(a):
    high = a.astype(BF16)
    return high, (a - high.astype(F32)).astype(BF16)


def dot3(a, b):
    return dot(a[0], b[0]) + (dot(a[1], b[0]) + dot(a[0], b[1]))


class Ring:
    def __init__(self, n, place, device_at, slot, send, recv):
        self.n, self.place, self.device_at, self.slot = n, place, device_at, slot
        self.send, self.recv = send, recv

    def parts(self, hop, way):
        return (way,) if hop == self.n // 2 - 1 else (0, 1)

    def copy(self, hop, way, part, arriving):
        n, sign = self.n, (1, -1)[way]
        owner = lax.rem(self.place + 2 * n - sign * (hop + arriving), n)
        block = self.slot(owner, part)
        return pltpu.make_async_remote_copy(
            src_ref=block,
            dst_ref=block,
            send_sem=self.send.at[way, hop, part],
            recv_sem=self.recv.at[way, hop, part],
            device_id=self.device_at(lax.rem(self.place + n + sign, n)),
            device_id_type=MESH,
        )

    def hop(self, hop):
        if hop > self.n // 2:
            return
        for part in (0, 1):
            for way in (0, 1):
                if hop > 0 and part in self.parts(hop - 1, way):
                    self.copy(hop - 1, way, part, 1).wait_recv()
                if hop < self.n // 2 and part in self.parts(hop, way):
                    self.copy(hop, way, part, 0).start()

    def finish(self):
        for hop in range(self.n // 2):
            for way in (0, 1):
                for part in self.parts(hop, way):
                    self.copy(hop, way, part, 0).wait_send()


def kernel(
    nz, ny, nh,
    q_hbm, k_hbm, v_hbm, b_hbm, w_hbm, o_ref,
    q_ref, k_ref, v_ref, b_ref, w_ref, k_int, v_int, wa, wb, pay_out, pay_in, m_out, m_in, e_all, s_pre, s_out, s_in, h_all,
    load_sem, a_send, a_recv, b_send, b_recv, wa_send, wa_recv, wb_send, wb_recv,
    d_send, d_recv, m_send, m_recv, s_send, s_recv, x_send, x_recv, c_send, c_recv,
):
    seq, head = lax.axis_index("seq"), lax.axis_index("head")
    z, y = seq // ny, lax.rem(seq, ny)
    x, core = head // 2, lax.rem(head, 2)
    nx = nh // 2
    heads = b_ref.shape[1]
    toks = q_ref.shape[0]
    dk = q_ref.shape[1] // heads
    refl = 2 * toks
    per = ny // heads
    sl = dk // per
    off_diagonal = z != head
    sibling = (seq, x * 2 + 1 - core)

    def on_y(i):
        return (z * ny + i, head)

    def on_z(i):
        return (i * ny + y, head)

    def signal(device):
        pl.semaphore_signal(barrier, inc=1, device_id=device, device_id_type=MESH)

    barrier = pltpu.get_barrier_semaphore()
    for d in range(1, ny):
        signal(on_y(lax.rem(y + d, ny)))
    for d in range(1, nz):
        signal(on_z(lax.rem(z + d, nz)))
    for d in range(1, nx):
        signal((seq, lax.rem(x + d, nx) * 2 + core))
    signal(sibling)
    for i in range(ny):

        @pl.when(off_diagonal | (i != y))
        def _():
            signal((head * ny + i, z))

    for i in range(nh):

        @pl.when(off_diagonal | (i != head))
        def _():
            signal((head * ny + y, i))

    loads = [
        pltpu.make_async_copy(src, dst, load_sem.at[n])
        for n, (src, dst) in enumerate(
            ((k_hbm, k_ref), (b_hbm, b_ref), (v_hbm, v_ref), (w_hbm, w_ref), (q_hbm, q_ref))
        )
    ]
    for load in loads:
        load.start()
    others = (ny - 1) + (nz - 1) + (nx - 1) + 1 + ny + nz
    pl.semaphore_wait(barrier, jnp.where(off_diagonal, others, others - 2))

    def half_a(i, arriving):
        return pltpu.make_async_remote_copy(
            src_ref=w_ref.at[:, pl.ds(0, dk)],
            dst_ref=wa.at[z, i] if arriving else wa.at[head, y],
            send_sem=a_send.at[i],
            recv_sem=a_recv.at[i if arriving else y],
            device_id=(head * ny + i, z),
            device_id_type=MESH,
        )

    def half_b(i, arriving):
        return pltpu.make_async_remote_copy(
            src_ref=w_ref.at[:, pl.ds(dk, dk)],
            dst_ref=wb.at[y, i if arriving else head],
            send_sem=b_send.at[i],
            recv_sem=b_recv.at[i if arriving else head],
            device_id=(i * ny + y, z),
            device_id_type=MESH,
        )

    def spread(action):
        for i in range(ny):

            @pl.when(off_diagonal | (i != y))
            def _():
                action(half_a, i)

        for i in range(nz):

            @pl.when(off_diagonal | (i != z))
            def _():
                action(half_b, i)

    loads[3].wait()
    spread(lambda half, i: half(i, 0).start())

    @pl.when(jnp.logical_not(off_diagonal))
    def _():
        wa[z, y] = w_ref[:, :dk]
        wb[y, z] = w_ref[:, dk:]

    wa_ring = Ring(nz, z, on_z, lambda i, p: wa.at[i, pl.ds(p * (ny // 2), ny // 2)], wa_send, wa_recv)
    wb_ring = Ring(ny, y, on_y, lambda i, p: wb.at[i, pl.ds(p * (nz // 2), nz // 2)], wb_send, wb_recv)

    def to_y(i, out, into, send, recv, arriving):
        return pltpu.make_async_remote_copy(
            src_ref=out.at[i],
            dst_ref=into.at[i if arriving else y],
            send_sem=send.at[i],
            recv_sem=recv.at[i if arriving else y],
            device_id=on_y(i),
            device_id_type=MESH,
        )

    def around_y(action):
        for i in range(ny):

            @pl.when(i != y)
            def _():
                action(i)

    def to_z(i, arriving):
        return pltpu.make_async_remote_copy(
            src_ref=m_out,
            dst_ref=m_in.at[i if arriving else z],
            send_sem=m_send.at[i],
            recv_sem=m_recv.at[i if arriving else z],
            device_id=on_z(i),
            device_id_type=MESH,
        )

    loads[0].wait()
    loads[1].wait()
    tok_id = lax.broadcasted_iota(jnp.int32, (refl, toks), 1)
    row_of = lax.broadcasted_iota(jnp.int32, (refl, toks), 0)
    ri = lax.broadcasted_iota(jnp.int32, (refl, refl), 0)
    ci = lax.broadcasted_iota(jnp.int32, (refl, refl), 1)
    keys, systems, gains, scales = [], [], [], []
    for h in range(heads):
        for j in (0, 1):
            k_int[h, pl.ds(j, toks, stride=2), :] = k_ref[j, :, h * dk : (h + 1) * dk].astype(F32)
    for h in range(heads):
        key = k_int[h]
        inv = lax.rsqrt(jnp.sum(key * key, axis=1, keepdims=True) + 1e-06)
        picked = jnp.where(
            lax.rem(row_of, 2) == 0, b_ref[0, h : h + 1, :], b_ref[1, h : h + 1, :]
        )
        beta = jnp.sum(jnp.where(row_of // 2 == tok_id, picked, 0.0), axis=1, keepdims=True)
        scales.append(beta * inv)
        gains.append(beta * inv * inv)
        kb = key.astype(BF16)
        keys.append(kb)
        systems.append(jnp.where(ri > ci, gains[h] * dot_nt(kb, kb), 0.0))
    eye = (ri == ci).astype(F32)
    inverses = [eye - jnp.where((ri >> 1) == (ci >> 1), a, 0.0) for a in systems]
    level = 1
    while (1 << level) < refl:
        here = ((ri >> (level + 1)) == (ci >> (level + 1))) & ((ri >> level) != (ci >> level))
        for h in range(heads):
            xb = inverses[h].astype(BF16)
            inner = dot(jnp.where(here, systems[h], 0.0).astype(BF16), xb)
            inverses[h] = inverses[h] - dot(xb, inner.astype(BF16))
        level += 1
    loads[2].wait()
    for h in range(heads):
        for j in (0, 1):
            v_int[h, pl.ds(j, toks, stride=2), :] = v_ref[j, :, h * dk : (h + 1) * dk].astype(F32)
    solved = []
    for h in range(heads):
        xs = split(inverses[h])
        residual = (eye - inverses[h]) - dot3(split(systems[h]), xs)
        fine = split(inverses[h] + dot(xs[0], residual.astype(BF16)))
        sides = jnp.concatenate([gains[h] * k_int[h], scales[h] * v_int[h]], axis=1)
        solved.append(dot3(fine, split(sides)))
    for h in range(heads):
        sh, slo = split(solved[h])
        moved = (dot_tn(sh, keys[h]) + dot_tn(slo, keys[h])).astype(BF16)
        for i in range(h, ny, heads):
            part = i // heads
            pay_out[i, :dk] = moved[:dk]
            pay_out[i, dk:] = moved[dk + part * sl : dk + (part + 1) * sl]
    around_y(lambda i: to_y(i, pay_out, pay_in, d_send, d_recv, 0).start())
    pay_in[y] = pay_out[y]
    for i in range(ny):

        @pl.when(off_diagonal | (i != y))
        def _():
            half_a(i, 1).wait_recv()

    wa_ring.hop(0)

    loads[4].wait()
    reach = (
        lax.broadcasted_iota(jnp.int32, (toks, refl), 1)
        <= 2 * lax.broadcasted_iota(jnp.int32, (toks, refl), 0) + 1
    )
    reads, locals_, q_inv = [], [], []
    for h in range(heads):
        qb = q_ref[:, h * dk : (h + 1) * dk]
        qf = qb.astype(F32)
        q_inv.append(lax.rsqrt(jnp.sum(qf * qf, axis=1, keepdims=True) + 1e-06))
        scores = jnp.where(reach, dot_nt(qb, keys[h]), 0.0)
        both = dot3(split(scores), split(solved[h]))
        reads.append((qf - both[:, :dk]).astype(BF16))
        locals_.append(both[:, dk:])

    top = (
        lax.broadcasted_iota(jnp.int32, (dk + sl, dk), 0)
        == lax.broadcasted_iota(jnp.int32, (dk + sl, dk), 1)
    ).astype(F32)
    bottom = lax.broadcasted_iota(jnp.int32, (dk + sl, dk), 0) >= dk
    stack = jnp.zeros((dk + sl, dk), F32)
    for i in range(ny):

        @pl.when(i != y)
        def _():
            to_y(i, pay_out, pay_in, d_send, d_recv, 1).wait_recv()

        e_all[:, i * dk : (i + 1) * dk] = stack[:dk].astype(BF16)
        s_pre[i] = stack[dk:]
        block = pay_in[i]
        grown = jnp.where(bottom, block.astype(F32), 0.0)
        stack = stack + dot((top - stack).astype(BF16), block[:dk]) + grown
    m_out[...] = stack.astype(BF16)
    for i in range(1, nz):

        @pl.when(i > z)
        def _():
            to_z(i, 0).start()

    wa_ring.hop(1)
    for i in range(nh):

        @pl.when(off_diagonal | (i != head))
        def _():
            half_b(i, 1).wait_recv()

    wb_ring.hop(0)
    state = jnp.zeros((sl, dk), F32)
    for i in range(nz - 1):

        @pl.when(i < z)
        def _():
            to_z(i, 1).wait_recv()

        block = m_in[i]
        after = state - dot(state.astype(BF16), block[:dk]) + block[dk:].astype(F32)
        state = jnp.where(i < z, after, state)
    drop = dot(state.astype(BF16), e_all[...])
    for i in range(ny):
        s_out[i] = (state - drop[:, i * dk : (i + 1) * dk] + s_pre[i]).astype(BF16)
    around_y(lambda i: to_y(i, s_out, s_in, s_send, s_recv, 0).start())
    s_in[y] = s_out[y]
    wa_ring.hop(2)
    wb_ring.hop(1)
    around_y(lambda i: to_y(i, s_out, s_in, s_send, s_recv, 1).wait_recv())

    def to_x(d, h, arriving):
        block = h_all.at[lax.rem(x + nx - d, nx) * 2 + core if arriving else head, h]
        return pltpu.make_async_remote_copy(
            src_ref=block,
            dst_ref=block,
            send_sem=x_send.at[d, h],
            recv_sem=x_recv.at[d, h],
            device_id=(seq, lax.rem(x + d, nx) * 2 + core),
            device_id_type=MESH,
        )

    def across(d, h, arriving):
        block = h_all.at[lax.rem(x + nx - d, nx) * 2 + (1 - core if arriving else core), h]
        return pltpu.make_async_remote_copy(
            src_ref=block,
            dst_ref=block,
            send_sem=c_send.at[d, h],
            recv_sem=c_recv.at[d, h],
            device_id=sibling,
            device_id_type=MESH,
        )

    distances = sorted(range(1, nx), key=lambda d: min(d, nx - d))
    for h in range(heads):
        carried = jnp.concatenate([s_in[i] for i in range(h, ny, heads)], axis=0)
        h_all[head, h] = (q_inv[h] * (dot_nt(reads[h], carried) + locals_[h])).astype(BF16)
        for d in distances:
            to_x(d, h, 0).start()
        across(0, h, 0).start()
    wa_ring.hop(3)
    wb_ring.hop(2)
    for d in distances:
        for h in range(heads):
            to_x(d, h, 1).wait_recv()
            across(d, h, 0).start()
    wb_ring.hop(3)
    wa_ring.hop(4)
    for d in [0] + distances:
        for h in range(heads):
            across(d, h, 1).wait_recv()
    wb_ring.hop(4)
    total = None
    for i in range(nh):
        left = jnp.concatenate([h_all[i, h] for h in range(heads)], axis=1)
        right = jnp.concatenate([wa[i].reshape(-1, dk), wb[:, i].reshape(-1, dk)], axis=1)
        term = dot_nt(left, right)
        total = term if total is None else total + term
    o_ref[...] = total.astype(BF16)

    spread(lambda half, i: half(i, 0).wait_send())
    wa_ring.finish()
    wb_ring.finish()
    around_y(lambda i: to_y(i, pay_out, pay_in, d_send, d_recv, 0).wait_send())
    around_y(lambda i: to_y(i, s_out, s_in, s_send, s_recv, 0).wait_send())
    for i in range(1, nz):

        @pl.when(i > z)
        def _():
            to_z(i, 0).wait_send()

    for h in range(heads):
        for d in distances:
            to_x(d, h, 0).wait_send()
        for d in [0] + distances:
            across(d, h, 0).wait_send()


def solution(mesh):
    nh = mesh.shape["head"]
    nz = nh
    ny = mesh.shape["seq"] // nz
    nx = nh // 2

    def per_device(queries, key_vectors, values, strengths, out_weight):
        toks = queries.shape[0]
        heads = strengths.shape[1]
        dk = queries.shape[1] // heads
        cols = out_weight.shape[1]
        sl = dk // (ny // heads)
        vmem, dma = pltpu.VMEM, pltpu.SemaphoreType.DMA

        def ring(n):
            return [dma((2, n // 2, 2))] * 2

        return pl.pallas_call(
            functools.partial(kernel, nz, ny, nh),
            out_shape=jax.ShapeDtypeStruct((toks, ny * cols), BF16),
            in_specs=[pl.BlockSpec(memory_space=pl.ANY)] * 5,
            out_specs=pl.BlockSpec(memory_space=pltpu.VMEM),
            scratch_shapes=[
                vmem(queries.shape, BF16),
                vmem(key_vectors.shape, BF16),
                vmem(values.shape, BF16),
                vmem(strengths.shape, F32),
                vmem((cols, heads * dk), BF16),
                vmem((heads, 2 * toks, dk), F32),
                vmem((heads, 2 * toks, dk), F32),
                vmem((nz, ny, cols, dk), BF16),
                vmem((ny, nz, cols, dk), BF16),
                vmem((ny, dk + sl, dk), BF16),
                vmem((ny, dk + sl, dk), BF16),
                vmem((dk + sl, dk), BF16),
                vmem((nz, dk + sl, dk), BF16),
                vmem((dk, ny * dk), BF16),
                vmem((ny, sl, dk), F32),
                vmem((ny, sl, dk), BF16),
                vmem((ny, sl, dk), BF16),
                vmem((nh, heads, toks, dk), BF16),
                dma((5,)),
                dma((ny,)),
                dma((ny,)),
                dma((nz,)),
                dma((nh,)),
                *ring(nz),
                *ring(ny),
                dma((ny,)),
                dma((ny,)),
                dma((nz,)),
                dma((nz,)),
                dma((ny,)),
                dma((ny,)),
                dma((nx, heads)),
                dma((nx, heads)),
                dma((nx, heads)),
                dma((nx, heads)),
            ],
            compiler_params=pltpu.CompilerParams(
                collective_id=0, has_side_effects=True, vmem_limit_bytes=62 * 1024 * 1024
            ),
        )(queries, key_vectors, values, strengths, out_weight.T)

    return jax.shard_map(
        per_device,
        mesh=mesh,
        in_specs=(
            P("seq", "head"),
            P(None, "seq", "head"),
            P(None, "seq", "head"),
            P(None, "head", "seq"),
            P("head", "seq"),
        ),
        out_specs=P("seq", "head"),
        check_vma=False,
    )
```

time: 99.1 us -> 58.3 us (0.59)
  the two profiles are of different devices: /device:TPU:7 before, /device:TPU:60 now
where the time goes in v2:
time: 58.3 us; the launch traced here: 58.2 us
  Pallas kernels  56.6 us (97%)
  local copies, waits for them, and re-layouts  1.57 us (3%)
    pallas_call x1, Pallas kernels, per_device(): pl.pallas_call(functools.partial(kernel, nz, ny, nh), out_shape=jax.Shape...  56.6 us
    unnamed x1, local copies, waits for them, and re-layouts  1.57 us

profile of v2, /device:TPU:60, one launch (start us, length us, event | category | flops | bytes accessed | tf_op | source)
XLA Modules:
  0.0 58.2 jit_solution(581142618284208278)
XLA Ops:
  0.0 56.6 %shard_map.55 = bf16[128,512]{1,0:T(8,128)(2,1)} custom-call(bf16[128,256]{1,0:T(8,128)(2,1)} %q_hbm.1, bf16[2,128,256]{2,1,0:T(8,128)(2,1)} %k_hbm.1, bf16[2,128,256]{2,1,0:T(8,128)(2,1)} %v_hbm.1, f32[2,2,128]{2,1,0:T(2,128)} %b_hbm.1, bf16[64,256]{1,0:T(8,128)(2,1)} %bitcast.1), custom_call_target="tpu_custom_call" | custom-call | tf_op jit(solution)/shard_map/pallas_call | solution.py:415
  56.6 1.6 %copy.7 = bf16[128,512]{1,0:T(8,128)(2,1)} copy(bf16[128,512]{1,0:T(8,128)(2,1)} %shard_map.55) | data formatting | bytes 262144

commit v3 on v2

--- a/solution.py
+++ b/solution.py
@@ -31,6 +31,10 @@
 
 def dot3(a, b):
     return dot(a[0], b[0]) + (dot(a[1], b[0]) + dot(a[0], b[1]))
+
+
+def far_first(n):
+    return sorted(range(1, n), key=lambda d: -min(d, n - d))
 
 
 class Ring:
@@ -108,17 +112,15 @@
     for d in range(1, nx):
         signal((seq, lax.rem(x + d, nx) * 2 + core))
     signal(sibling)
-    for i in range(ny):
-
-        @pl.when(off_diagonal | (i != y))
-        def _():
-            signal((head * ny + i, z))
-
-    for i in range(nh):
-
-        @pl.when(off_diagonal | (i != head))
-        def _():
-            signal((head * ny + y, i))
+    for d in range(1, ny):
+        signal((head * ny + lax.rem(y + d, ny), z))
+    for d in range(1, nh):
+        signal((head * ny + y, lax.rem(z + d, nh)))
+
+    @pl.when(off_diagonal)
+    def _():
+        signal((head * ny + y, z))
+        signal((head * ny + y, z))
 
     loads = [
         pltpu.make_async_copy(src, dst, load_sem.at[n])
@@ -131,41 +133,41 @@
     others = (ny - 1) + (nz - 1) + (nx - 1) + 1 + ny + nz
     pl.semaphore_wait(barrier, jnp.where(off_diagonal, others, others - 2))
 
-    def half_a(i, arriving):
+    def half_a(d, arriving):
+        other = lax.rem(y + ny - d, ny)
         return pltpu.make_async_remote_copy(
             src_ref=w_ref.at[:, pl.ds(0, dk)],
-            dst_ref=wa.at[z, i] if arriving else wa.at[head, y],
-            send_sem=a_send.at[i],
-            recv_sem=a_recv.at[i if arriving else y],
-            device_id=(head * ny + i, z),
-            device_id_type=MESH,
-        )
-
-    def half_b(i, arriving):
+            dst_ref=wa.at[z, other] if arriving else wa.at[head, y],
+            send_sem=a_send.at[d],
+            recv_sem=a_recv.at[d],
+            device_id=(head * ny + lax.rem(y + d, ny), z),
+            device_id_type=MESH,
+        )
+
+    def half_b(d, arriving):
+        other = lax.rem(z + nz - d, nz)
         return pltpu.make_async_remote_copy(
             src_ref=w_ref.at[:, pl.ds(dk, dk)],
-            dst_ref=wb.at[y, i if arriving else head],
-            send_sem=b_send.at[i],
-            recv_sem=b_recv.at[i if arriving else head],
-            device_id=(i * ny + y, z),
-            device_id_type=MESH,
-        )
-
-    def spread(action):
-        for i in range(ny):
-
-            @pl.when(off_diagonal | (i != y))
-            def _():
-                action(half_a, i)
-
-        for i in range(nz):
-
-            @pl.when(off_diagonal | (i != z))
-            def _():
-                action(half_b, i)
-
+            dst_ref=wb.at[y, other if arriving else head],
+            send_sem=b_send.at[d],
+            recv_sem=b_recv.at[d],
+            device_id=(lax.rem(head + d, nz) * ny + y, z),
+            device_id_type=MESH,
+        )
+
+    def spread(action, copies):
+        for half, n in copies:
+            for d in far_first(n):
+                action(half, d)
+
+        @pl.when(off_diagonal)
+        def _():
+            for half, _ in copies:
+                action(half, 0)
+
+    both_halves = ((half_a, ny), (half_b, nz))
     loads[3].wait()
-    spread(lambda half, i: half(i, 0).start())
+    spread(lambda half, d: half(d, 0).start(), both_halves)
 
     @pl.when(jnp.logical_not(off_diagonal))
     def _():
@@ -175,22 +177,20 @@
     wa_ring = Ring(nz, z, on_z, lambda i, p: wa.at[i, pl.ds(p * (ny // 2), ny // 2)], wa_send, wa_recv)
     wb_ring = Ring(ny, y, on_y, lambda i, p: wb.at[i, pl.ds(p * (nz // 2), nz // 2)], wb_send, wb_recv)
 
-    def to_y(i, out, into, send, recv, arriving):
-        return pltpu.make_async_remote_copy(
-            src_ref=out.at[i],
-            dst_ref=into.at[i if arriving else y],
-            send_sem=send.at[i],
-            recv_sem=recv.at[i if arriving else y],
-            device_id=on_y(i),
+    def to_y(d, out, into, send, recv, arriving):
+        peer, other = lax.rem(y + d, ny), lax.rem(y + ny - d, ny)
+        return pltpu.make_async_remote_copy(
+            src_ref=out.at[peer],
+            dst_ref=into.at[other if arriving else y],
+            send_sem=send.at[d],
+            recv_sem=recv.at[d],
+            device_id=on_y(peer),
             device_id_type=MESH,
         )
 
     def around_y(action):
-        for i in range(ny):
-
-            @pl.when(i != y)
-            def _():
-                action(i)
+        for d in far_first(ny):
+            action(d)
 
     def to_z(i, arriving):
         return pltpu.make_async_remote_copy(
@@ -225,15 +225,33 @@
         keys.append(kb)
         systems.append(jnp.where(ri > ci, gains[h] * dot_nt(kb, kb), 0.0))
     eye = (ri == ci).astype(F32)
-    inverses = [eye - jnp.where((ri >> 1) == (ci >> 1), a, 0.0) for a in systems]
+    half = refl // 2
+    ri2, ci2, eye2 = ri[:half, :half], ci[:half, :half], eye[:half, :half]
+    blocks = [a[o : o + half, o : o + half] for a in systems for o in (0, half)]
+    parts = [eye2 - jnp.where((ri2 >> 1) == (ci2 >> 1), a, 0.0) for a in blocks]
     level = 1
-    while (1 << level) < refl:
-        here = ((ri >> (level + 1)) == (ci >> (level + 1))) & ((ri >> level) != (ci >> level))
-        for h in range(heads):
-            xb = inverses[h].astype(BF16)
-            inner = dot(jnp.where(here, systems[h], 0.0).astype(BF16), xb)
-            inverses[h] = inverses[h] - dot(xb, inner.astype(BF16))
+    while (1 << level) < half:
+        here = ((ri2 >> (level + 1)) == (ci2 >> (level + 1))) & ((ri2 >> level) != (ci2 >> level))
+        narrow = [p.astype(BF16) for p in parts]
+        inner = [
+            dot(jnp.where(here, a, 0.0).astype(BF16), p) for a, p in zip(blocks, narrow)
+        ]
+        parts = [p - dot(b, i.astype(BF16)) for p, b, i in zip(parts, narrow, inner)]
         level += 1
+    inverses = []
+    for h in range(heads):
+        first, second = parts[2 * h], parts[2 * h + 1]
+        inner = dot(systems[h][half:, :half].astype(BF16), first.astype(BF16))
+        corner = -dot(second.astype(BF16), inner.astype(BF16))
+        inverses.append(
+            jnp.concatenate(
+                [
+                    jnp.concatenate([first, jnp.zeros_like(first)], axis=1),
+                    jnp.concatenate([corner, second], axis=1),
+                ],
+                axis=0,
+            )
+        )
     loads[2].wait()
     for h in range(heads):
         for j in (0, 1):
@@ -252,16 +270,8 @@
             part = i // heads
             pay_out[i, :dk] = moved[:dk]
             pay_out[i, dk:] = moved[dk + part * sl : dk + (part + 1) * sl]
-    around_y(lambda i: to_y(i, pay_out, pay_in, d_send, d_recv, 0).start())
+    around_y(lambda d: to_y(d, pay_out, pay_in, d_send, d_recv, 0).start())
     pay_in[y] = pay_out[y]
-    for i in range(ny):
-
-        @pl.when(off_diagonal | (i != y))
-        def _():
-            half_a(i, 1).wait_recv()
-
-    wa_ring.hop(0)
-
     loads[4].wait()
     reach = (
         lax.broadcasted_iota(jnp.int32, (toks, refl), 1)
@@ -277,56 +287,77 @@
         reads.append((qf - both[:, :dk]).astype(BF16))
         locals_.append(both[:, dk:])
 
+    spread(lambda half, d: half(d, 1).wait_recv(), both_halves[:1])
+    wa_ring.hop(0)
     top = (
         lax.broadcasted_iota(jnp.int32, (dk + sl, dk), 0)
         == lax.broadcasted_iota(jnp.int32, (dk + sl, dk), 1)
     ).astype(F32)
     bottom = lax.broadcasted_iota(jnp.int32, (dk + sl, dk), 0) >= dk
-    stack = jnp.zeros((dk + sl, dk), F32)
+
+    def join(earlier, later):
+        moved = dot((top - earlier).astype(BF16), later[:dk].astype(BF16))
+        return earlier + moved + jnp.where(bottom, later, 0.0)
+
+    def prefixes(terms):
+        done = [terms[0]]
+        for term in terms[1:]:
+            done.append(join(done[-1], term))
+        return done
+
+    around = far_first(ny)[::-1]
+    for n, d in enumerate(around):
+        to_y(d, pay_out, pay_in, d_send, d_recv, 1).wait_recv()
+    spread(lambda half, d: half(d, 1).wait_recv(), both_halves[1:])
+    wb_ring.hop(0)
+    upto = prefixes([pay_in[i].astype(F32) for i in range(ny)])
+    m_out[...] = upto[-1].astype(BF16)
+    for d in range(nz - 1, 0, -1):
+
+        @pl.when(z + d < nz)
+        def _():
+            to_z(z + d, 0).start()
+
+    wa_ring.hop(1)
+
     for i in range(ny):
-
-        @pl.when(i != y)
-        def _():
-            to_y(i, pay_out, pay_in, d_send, d_recv, 1).wait_recv()
-
+        stack = upto[i - 1] if i > 0 else jnp.zeros((dk + sl, dk), F32)
         e_all[:, i * dk : (i + 1) * dk] = stack[:dk].astype(BF16)
         s_pre[i] = stack[dk:]
-        block = pay_in[i]
-        grown = jnp.where(bottom, block.astype(F32), 0.0)
-        stack = stack + dot((top - stack).astype(BF16), block[:dk]) + grown
-    m_out[...] = stack.astype(BF16)
-    for i in range(1, nz):
-
-        @pl.when(i > z)
-        def _():
-            to_z(i, 0).start()
-
-    wa_ring.hop(1)
-    for i in range(nh):
-
-        @pl.when(off_diagonal | (i != head))
-        def _():
-            half_b(i, 1).wait_recv()
-
-    wb_ring.hop(0)
-    state = jnp.zeros((sl, dk), F32)
+    wb_ring.hop(1)
     for i in range(nz - 1):
 
         @pl.when(i < z)
         def _():
             to_z(i, 1).wait_recv()
 
-        block = m_in[i]
-        after = state - dot(state.astype(BF16), block[:dk]) + block[dk:].astype(F32)
-        state = jnp.where(i < z, after, state)
+    rows_in = [jnp.where(i < z, m_in[i].astype(F32), 0.0) for i in range(nz - 1)]
+
+    def middle_of(terms):
+        return 1 << ((len(terms) - 1).bit_length() - 1)
+
+    def whole(terms):
+        if len(terms) == 1:
+            return terms[0]
+        middle = middle_of(terms)
+        return join(whole(terms[:middle]), whole(terms[middle:]))
+
+    def state_after(terms):
+        if len(terms) == 1:
+            return terms[0][dk:]
+        middle = middle_of(terms)
+        earlier, later = state_after(terms[:middle]), whole(terms[middle:])
+        return earlier - dot(earlier.astype(BF16), later[:dk].astype(BF16)) + later[dk:]
+
+    state = state_after(rows_in)
     drop = dot(state.astype(BF16), e_all[...])
     for i in range(ny):
         s_out[i] = (state - drop[:, i * dk : (i + 1) * dk] + s_pre[i]).astype(BF16)
-    around_y(lambda i: to_y(i, s_out, s_in, s_send, s_recv, 0).start())
+    around_y(lambda d: to_y(d, s_out, s_in, s_send, s_recv, 0).start())
     s_in[y] = s_out[y]
     wa_ring.hop(2)
-    wb_ring.hop(1)
-    around_y(lambda i: to_y(i, s_out, s_in, s_send, s_recv, 1).wait_recv())
+    wb_ring.hop(2)
+    around_y(lambda d: to_y(d, s_out, s_in, s_send, s_recv, 1).wait_recv())
 
     def to_x(d, h, arriving):
         block = h_all.at[lax.rem(x + nx - d, nx) * 2 + core if arriving else head, h]
@@ -350,38 +381,43 @@
             device_id_type=MESH,
         )
 
-    distances = sorted(range(1, nx), key=lambda d: min(d, nx - d))
+    distances = far_first(nx)
     for h in range(heads):
         carried = jnp.concatenate([s_in[i] for i in range(h, ny, heads)], axis=0)
         h_all[head, h] = (q_inv[h] * (dot_nt(reads[h], carried) + locals_[h])).astype(BF16)
         for d in distances:
             to_x(d, h, 0).start()
         across(0, h, 0).start()
+    distances = distances[::-1]
     wa_ring.hop(3)
-    wb_ring.hop(2)
+    wb_ring.hop(3)
     for d in distances:
         for h in range(heads):
             to_x(d, h, 1).wait_recv()
             across(d, h, 0).start()
-    wb_ring.hop(3)
     wa_ring.hop(4)
+    wb_ring.hop(4)
+
+    def term(d, which):
+        i = lax.rem(x + nx - d, nx) * 2 + which
+        left = jnp.concatenate([h_all[i, h] for h in range(heads)], axis=1)
+        right = jnp.concatenate([wa[i].reshape(-1, dk), wb[:, i].reshape(-1, dk)], axis=1)
+        return dot_nt(left, right)
+
+    total = term(0, core)
+    for d in distances:
+        total = total + term(d, core)
     for d in [0] + distances:
         for h in range(heads):
             across(d, h, 1).wait_recv()
-    wb_ring.hop(4)
-    total = None
-    for i in range(nh):
-        left = jnp.concatenate([h_all[i, h] for h in range(heads)], axis=1)
-        right = jnp.concatenate([wa[i].reshape(-1, dk), wb[:, i].reshape(-1, dk)], axis=1)
-        term = dot_nt(left, right)
-        total = term if total is None else total + term
+        total = total + term(d, 1 - core)
     o_ref[...] = total.astype(BF16)
 
-    spread(lambda half, i: half(i, 0).wait_send())
+    spread(lambda half, d: half(d, 0).wait_send(), both_halves)
     wa_ring.finish()
     wb_ring.finish()
-    around_y(lambda i: to_y(i, pay_out, pay_in, d_send, d_recv, 0).wait_send())
-    around_y(lambda i: to_y(i, s_out, s_in, s_send, s_recv, 0).wait_send())
+    around_y(lambda d: to_y(d, pay_out, pay_in, d_send, d_recv, 0).wait_send())
+    around_y(lambda d: to_y(d, s_out, s_in, s_send, s_recv, 0).wait_send())
     for i in range(1, nz):
 
         @pl.when(i > z)

time: 58.3 us -> 54.1 us (0.928)
  the two profiles are of different devices: /device:TPU:60 before, /device:TPU:8 now
where the time goes in v3:
time: 54.1 us; the launch traced here: 53.9 us
  Pallas kernels  52.4 us (97%)
  local copies, waits for them, and re-layouts  1.57 us (3%)
    pallas_call x1, Pallas kernels, per_device(): pl.pallas_call(functools.partial(kernel, nz, ny, nh), out_shape=jax.Shape...  52.4 us
    unnamed x1, local copies, waits for them, and re-layouts  1.57 us

profile of v3, /device:TPU:8, one launch (start us, length us, event | category | flops | bytes accessed | tf_op | source)
XLA Modules:
  0.0 53.9 jit_solution(9229874727654842335)
XLA Ops:
  0.0 52.4 %shard_map.55 = bf16[128,512]{1,0:T(8,128)(2,1)} custom-call(bf16[128,256]{1,0:T(8,128)(2,1)} %q_hbm.1, bf16[2,128,256]{2,1,0:T(8,128)(2,1)} %k_hbm.1, bf16[2,128,256]{2,1,0:T(8,128)(2,1)} %v_hbm.1, f32[2,2,128]{2,1,0:T(2,128)} %b_hbm.1, bf16[64,256]{1,0:T(8,128)(2,1)} %bitcast.1), custom_call_target="tpu_custom_call" | custom-call | tf_op jit(solution)/shard_map/pallas_call | solution.py:451
  52.4 1.6 %copy.7 = bf16[128,512]{1,0:T(8,128)(2,1)} copy(bf16[128,512]{1,0:T(8,128)(2,1)} %shard_map.55) | data formatting | bytes 262144

commit v4 on v3

--- a/solution.py
+++ b/solution.py
@@ -104,6 +104,15 @@
     def signal(device):
         pl.semaphore_signal(barrier, inc=1, device_id=device, device_id_type=MESH)
 
+    loads = [
+        pltpu.make_async_copy(src, dst, load_sem.at[n])
+        for n, (src, dst) in enumerate(
+            ((k_hbm, k_ref), (b_hbm, b_ref), (v_hbm, v_ref), (w_hbm, w_ref), (q_hbm, q_ref))
+        )
+    ]
+    for load in loads:
+        load.start()
+
     barrier = pltpu.get_barrier_semaphore()
     for d in range(1, ny):
         signal(on_y(lax.rem(y + d, ny)))
@@ -112,8 +121,6 @@
     for d in range(1, nx):
         signal((seq, lax.rem(x + d, nx) * 2 + core))
     signal(sibling)
-    for d in range(1, ny):
-        signal((head * ny + lax.rem(y + d, ny), z))
     for d in range(1, nh):
         signal((head * ny + y, lax.rem(z + d, nh)))
 
@@ -122,25 +129,20 @@
         signal((head * ny + y, z))
         signal((head * ny + y, z))
 
-    loads = [
-        pltpu.make_async_copy(src, dst, load_sem.at[n])
-        for n, (src, dst) in enumerate(
-            ((k_hbm, k_ref), (b_hbm, b_ref), (v_hbm, v_ref), (w_hbm, w_ref), (q_hbm, q_ref))
-        )
-    ]
-    for load in loads:
-        load.start()
-    others = (ny - 1) + (nz - 1) + (nx - 1) + 1 + ny + nz
-    pl.semaphore_wait(barrier, jnp.where(off_diagonal, others, others - 2))
-
     def half_a(d, arriving):
         other = lax.rem(y + ny - d, ny)
-        return pltpu.make_async_remote_copy(
-            src_ref=w_ref.at[:, pl.ds(0, dk)],
-            dst_ref=wa.at[z, other] if arriving else wa.at[head, y],
+        if d == 0:
+            src, dst = w_ref.at[:, pl.ds(0, dk)], wa.at[z, y] if arriving else wa.at[head, y]
+            device = (head * ny + y, z)
+        else:
+            src = dst = wa.at[z, other if arriving else y]
+            device = on_y(lax.rem(y + d, ny))
+        return pltpu.make_async_remote_copy(
+            src_ref=src,
+            dst_ref=dst,
             send_sem=a_send.at[d],
             recv_sem=a_recv.at[d],
-            device_id=(head * ny + lax.rem(y + d, ny), z),
+            device_id=device,
             device_id_type=MESH,
         )
 
@@ -165,15 +167,7 @@
             for half, _ in copies:
                 action(half, 0)
 
-    both_halves = ((half_a, ny), (half_b, nz))
-    loads[3].wait()
-    spread(lambda half, d: half(d, 0).start(), both_halves)
-
-    @pl.when(jnp.logical_not(off_diagonal))
-    def _():
-        wa[z, y] = w_ref[:, :dk]
-        wb[y, z] = w_ref[:, dk:]
-
+    both_halves = ((half_a, 1), (half_b, nz))
     wa_ring = Ring(nz, z, on_z, lambda i, p: wa.at[i, pl.ds(p * (ny // 2), ny // 2)], wa_send, wa_recv)
     wb_ring = Ring(ny, y, on_y, lambda i, p: wb.at[i, pl.ds(p * (nz // 2), nz // 2)], wb_send, wb_recv)
 
@@ -238,6 +232,17 @@
         ]
         parts = [p - dot(b, i.astype(BF16)) for p, b, i in zip(parts, narrow, inner)]
         level += 1
+    others = (ny - 1) + (nz - 1) + (nx - 1) + 1 + 1 + nz
+    pl.semaphore_wait(barrier, jnp.where(off_diagonal, others, others - 2))
+
+    loads[3].wait()
+    spread(lambda half, d: half(d, 0).start(), both_halves)
+
+    @pl.when(jnp.logical_not(off_diagonal))
+    def _():
+        wa[z, y] = w_ref[:, :dk]
+        wb[y, z] = w_ref[:, dk:]
+
     inverses = []
     for h in range(heads):
         first, second = parts[2 * h], parts[2 * h + 1]
@@ -272,6 +277,9 @@
             pay_out[i, dk:] = moved[dk + part * sl : dk + (part + 1) * sl]
     around_y(lambda d: to_y(d, pay_out, pay_in, d_send, d_recv, 0).start())
     pay_in[y] = pay_out[y]
+    spread(lambda half, d: half(d, 1).wait_recv(), both_halves[:1])
+    for d in far_first(ny):
+        half_a(d, 0).start()
     loads[4].wait()
     reach = (
         lax.broadcasted_iota(jnp.int32, (toks, refl), 1)
@@ -287,7 +295,8 @@
         reads.append((qf - both[:, :dk]).astype(BF16))
         locals_.append(both[:, dk:])
 
-    spread(lambda half, d: half(d, 1).wait_recv(), both_halves[:1])
+    for d in far_first(ny)[::-1]:
+        half_a(d, 1).wait_recv()
     wa_ring.hop(0)
     top = (
         lax.broadcasted_iota(jnp.int32, (dk + sl, dk), 0)
@@ -414,6 +423,8 @@
     o_ref[...] = total.astype(BF16)
 
     spread(lambda half, d: half(d, 0).wait_send(), both_halves)
+    for d in far_first(ny):
+        half_a(d, 0).wait_send()
     wa_ring.finish()
     wb_ring.finish()
     around_y(lambda d: to_y(d, pay_out, pay_in, d_send, d_recv, 0).wait_send())

time: 54.1 us -> 53.9 us (level)
  the two profiles are of different devices: /device:TPU:8 before, /device:TPU:2 now
where the time goes in v4:
time: 53.9 us; the launch traced here: 53.7 us
  Pallas kernels  52.1 us (97%)
  local copies, waits for them, and re-layouts  1.57 us (3%)
    pallas_call x1, Pallas kernels, per_device(): pl.pallas_call(functools.partial(kernel, nz, ny, nh), out_shape=jax.Shape...  52.1 us
    unnamed x1, local copies, waits for them, and re-layouts  1.57 us

profile of v4, /device:TPU:2, one launch (start us, length us, event | category | flops | bytes accessed | tf_op | source)
XLA Modules:
  0.0 53.7 jit_solution(17592713937219705976)
XLA Ops:
  0.0 52.1 %shard_map.55 = bf16[128,512]{1,0:T(8,128)(2,1)} custom-call(bf16[128,256]{1,0:T(8,128)(2,1)} %q_hbm.1, bf16[2,128,256]{2,1,0:T(8,128)(2,1)} %k_hbm.1, bf16[2,128,256]{2,1,0:T(8,128)(2,1)} %v_hbm.1, f32[2,2,128]{2,1,0:T(2,128)} %b_hbm.1, bf16[64,256]{1,0:T(8,128)(2,1)} %bitcast.1), custom_call_target="tpu_custom_call" | custom-call | tf_op jit(solution)/shard_map/pallas_call | solution.py:462
  52.1 1.6 %copy.7 = bf16[128,512]{1,0:T(8,128)(2,1)} copy(bf16[128,512]{1,0:T(8,128)(2,1)} %shard_map.55) | data formatting | bytes 262144
